TPU v7x, 256 devices: a whole 4x4x8 slice. The times are simulated.
256 devices in a mesh: band: 64 (over z, y, x_lo), kpt: 4 (over x_hi, core).
Axes of the slice: x: 4 (x_hi: 2, x_lo: 2; x = x_hi * 2 + x_lo), y: 4, z: 8, core: 2. Of those that a mesh axis runs over, the one named last changes fastest.
Arguments:
- orbitals: float32 [64, 4, 2, 32, 768], P('band', 'kpt'), may hold values from -6 to 6
- screened_kernel: float32 [4, 32, 768], replicated, may hold values from 0.1 to 4
- kpoint_index: int32 [4], replicated, may hold values from 0 to 15, as said below
- q_index: int32 [16, 16], replicated, may hold values from 0 to 3
Outputs:
- exchange: float32 [64, 4, 2, 32, 768], P('band', 'kpt')
Inputs may be any that keep to these rules, and one draw needn't show every extreme that they name: `kpoint_index`: the k-point numbers of the positions are all different.
All inputs are finite; a program needn't handle non-finite values.
Results may differ from a plain program's by a relative error of at most 0.0003.
Values sent between devices are 32-bit elements; how exact they have to be, the bound alone decides.
A program may use at most 64 MiB of HBM per device.

v0:
```python
import numpy as np, ml_dtypes
import jax, jax.numpy as jnp
from jax import lax
from jax.sharding import PartitionSpec as P
from jax.experimental import pallas as pl
from jax.experimental.pallas import tpu as pltpu
X,Y,Z=32,32,24
YZ=Y*Z; H=YZ//2
f32=jnp.float32; bf16=jnp.bfloat16

def split_np(a):
    hi=a.astype(np.float32).astype(ml_dtypes.bfloat16)
    lo=(a-hi.astype(np.float64)).astype(np.float32).astype(ml_dtypes.bfloat16)
    return hi,lo

def tables():
    y=np.arange(Y//2)[:,None,None,None]; z=np.arange(Z)[None,:,None,None]
    m=np.arange(Y//2)[None,None,:,None]; kz=np.arange(Z)[None,None,None,:]
    ws=[]
    for c in range(2):
        ph=(3*y*(2*m+c)+4*z*kz)%96
        th=2*np.pi*ph/96
        C=np.cos(th).reshape(H,H); S=np.sin(th).reshape(H,H)
        ws.append(np.block([[C,-S],[S,C]]))
    W=np.stack(ws)
    whi,wlo=split_np(W)
    xx=np.arange(X); th=2*np.pi*((xx[:,None]*xx[None,:])%X)/X
    C=np.cos(th);S=np.sin(th)
    F=np.block([[C,S],[-S,C]])
    I=np.block([[C,-S],[S,C]])
    def lhs(D):
        h,l=split_np(D); return np.concatenate([h,l,h],1)
    dx=np.stack([lhs(F),lhs(I)])
    perm=np.zeros((YZ,YZ),np.float32)
    for c in range(2):
        for mm in range(Y//2):
            for k in range(Z):
                perm[(2*mm+c)*Z+k, c*H+mm*Z+k]=1
    return whi,wlo,dx,perm.astype(ml_dtypes.bfloat16)

def split(a):
    hi=a.astype(bf16)
    lo=(a-hi.astype(f32)).astype(bf16)
    return hi,lo

def dotn(a,b): return jnp.dot(a,b,preferred_element_type=f32)
def dott(a,b): return lax.dot_general(a,b,(((1,),(1,)),((),())),preferred_element_type=f32)

def three(a,whi,wlo,dot):
    hi,lo=split(a)
    return dot(hi,whi)+dot(lo,whi)+dot(hi,wlo)

def group(res, vis_ref, first, G, kp_ref, whi, wlo, dx, acc, trans=True, koff=0):
    rr,ri=res
    s_rows=[];d_rows=[]
    for g in range(G):
        vr=vis_ref[first+g,0]; vi=vis_ref[first+g,1]
        pr=vr*rr+vi*ri; pi=vr*ri-vi*rr
        s_rows.append(jnp.concatenate([pr[:,:H]+pr[:,H:],pi[:,:H]+pi[:,H:]],1))
        d_rows.append(jnp.concatenate([pr[:,:H]-pr[:,H:],pi[:,:H]-pi[:,H:]],1))
    tS=three(jnp.concatenate(s_rows,0),whi[0],wlo[0],dotn)
    tD=three(jnp.concatenate(d_rows,0),whi[1],wlo[1],dotn)
    e_rows=[];o_rows=[]
    for g in range(G):
        rows=slice(g*X,g*X+X)
        a=jnp.concatenate([jnp.concatenate([tS[rows,:H],tD[rows,:H]],1),jnp.concatenate([tS[rows,H:],tD[rows,H:]],1)],0)
        hi,lo=split(a)
        sp=dotn(dx[0],jnp.concatenate([hi,hi,lo],0))
        k=kp_ref[koff+g]
        sp=sp*jnp.concatenate([k,k],0)
        hi,lo=split(sp)
        q=dotn(dx[1],jnp.concatenate([hi,hi,lo],0))
        e_rows.append(jnp.concatenate([q[:X,:H],q[X:,:H]],1))
        o_rows.append(jnp.concatenate([q[:X,H:],q[X:,H:]],1))
    uE=three(jnp.concatenate(e_rows,0),whi[0],wlo[0],dott)
    uO=three(jnp.concatenate(o_rows,0),whi[1],wlo[1],dott)
    for g in range(G):
        rows=slice(g*X,g*X+X)
        er,ei,orr,oi=uE[rows,:H],uE[rows,H:],uO[rows,:H],uO[rows,H:]
        pr=jnp.concatenate([er+orr,er-orr],1); pi=jnp.concatenate([ei+oi,ei-oi],1)
        vr=vis_ref[first+g,0]; vi=vis_ref[first+g,1]
        acc[0]+=vr*pr-vi*pi
        acc[1]+=vr*pi+vi*pr

def permute_k(kern_ref, kp_ref, kpt, q_ref, me, perm):
    own=kpt[me]
    rows=[kern_ref[q_ref[own,kpt[j]]] for j in range(4)]
    k=jnp.concatenate(rows,0)*(-1.0/(4*X*Y*Z))
    a=k.astype(bf16); r=k-a.astype(f32); b=r.astype(bf16); c=(r-b.astype(f32)).astype(bf16)
    out=dotn(a,perm)+dotn(b,perm)+dotn(c,perm)
    for j in range(4): kp_ref[j]=out[j*X:(j+1)*X]


def kernel(mid_ref, low_ref, high_ref, kern_ref, kpt, q, whi, wlo, dx, perm, out, kp, own):
    me = lax.axis_index("kpt")
    permute_k(kern_ref, kp, kpt, q, me, perm[...])
    own[...] = mid_ref[me]
    out[...] = jnp.zeros_like(out)
    for ref in (mid_ref, low_ref, high_ref):
        group((own[0], own[1]), ref, 0, 4, kp, whi, wlo, dx, out)


def local(orbitals, screened_kernel, kpoint_index, q_index):
    count = lax.axis_size("band")
    rows = lax.all_gather(orbitals[0, 0], "kpt", axis=0, tiled=False)
    low = lax.ppermute(rows, "band", [(i, (i + 1) % count) for i in range(count)])
    high = lax.ppermute(rows, "band", [((i + 1) % count, i) for i in range(count)])
    whi, wlo, dx, perm = tables()
    vmem = pl.BlockSpec(memory_space=pltpu.VMEM)
    smem = pl.BlockSpec(memory_space=pltpu.SMEM)
    out = pl.pallas_call(
        kernel,
        out_shape=jax.ShapeDtypeStruct((2, X, YZ), f32),
        in_specs=[vmem] * 4 + [smem] * 2 + [vmem] * 4,
        out_specs=vmem,
        scratch_shapes=[pltpu.VMEM((4, X, YZ), f32), pltpu.VMEM((2, X, YZ), f32)],
        compiler_params=pltpu.CompilerParams(vmem_limit_bytes=60 << 20),
        name="exchange",
    )(rows, low, high, screened_kernel, kpoint_index, q_index, whi, wlo, dx, perm)
    return out[None, None]


def solution(mesh):
    return jax.shard_map(
        local,
        mesh=mesh,
        in_specs=(P("band", "kpt", None, None, None), P(), P(), P()),
        out_specs=P("band", "kpt", None, None, None),
        check_vma=False,
    )
```

profile of v0, /device:TPU:1, one launch (start us, length us, event | category | flops | bytes accessed | tf_op | source)
XLA Modules:
  0.0 69.6 jit_solution(14941258552727681633)
XLA Ops:
  0.0 12.0 %all-gather = f32[4,1,2,32,768]{4,3,2,1,0:T(8,128)S(1)} all-gather(f32[1,1,2,32,768]{4,3,2,1,0:T(8,128)} %param.8), channel_id=2, replica_groups=mesh['band'=64,'kpt'=4] {'kpt'}, dimensions={0}, use_global_device_ids=true | all-gather | bytes 983040 | tf_op jit(solution)/shard_map/all_gather | solution.py:105
  12.0 0.0 copy-start
  12.0 8.2 %collective-permute-start.1 = (f32[4,2,32,768]{3,2,1,0:T(8,128)S(1)}, f32[4,2,32,768]{3,2,1,0:T(8,128)S(1)}, u32[]{:S(2)}, u32[]{:S(2)}) collective-permute-start(f32[4,2,32,768]{3,2,1,0:T(8,128)S(1)} %bitcast.2), channel_id=1, source_target_pairs={{4,0},{8,4},{12,8},{16,12},{20,16},{24,20},{28,24},{32,28},{36,32}... | collective-permute-start | bytes 2359304 | tf_op jit(solution)/shard_map/ppermute | solution.py:107
  20.2 0.0 collective-permute-start
  20.2 16.8 %collective-permute-done.1.high_ref = f32[4,2,32,768]{3,2,1,0:T(8,128)S(1)} collective-permute-done((f32[4,2,32,768]{3,2,1,0:T(8,128)S(1)}, f32[4,2,32,768]{3,2,1,0:T(8,128)S(1)}, u32[]{:S(2)}, u32[]{:S(2)}) %collective-permute-start.1) | collective-permute-done | bytes 786464 | tf_op jit(solution)/shard_map/ppermute | solution.py:107
  37.0 0.0 copy-start.1
  37.0 12.9 %collective-permute-done.low_ref = f32[4,2,32,768]{3,2,1,0:T(8,128)S(1)} collective-permute-done((f32[4,2,32,768]{3,2,1,0:T(8,128)S(1)}, f32[4,2,32,768]{3,2,1,0:T(8,128)S(1)}, u32[]{:S(2)}, u32[]{:S(2)}) %collective-permute-start) | collective-permute-done | bytes 786464 | tf_op jit(solution)/shard_map/ppermute | solution.py:106
  50.0 0.0 copy-done
  50.0 0.0 copy-done.1
  50.0 0.0 copy-start.2
  50.0 0.9 %copy-done.2 = f32[4,2,32,768]{3,2,1,0:T(8,128)} copy-done((f32[4,2,32,768]{3,2,1,0:T(8,128)}, f32[4,2,32,768]{3,2,1,0:T(8,128)S(1)}, u32[]{:S(2)}) %copy-start.2) | copy-done | bytes 786456
  50.9 18.7 %exchange.1 = f32[2,32,768]{2,1,0:T(8,128)} custom-call(f32[4,2,32,768]{3,2,1,0:T(8,128)} %bitcast.4, f32[4,2,32,768]{3,2,1,0:T(8,128)} %copy-done.2, f32[4,2,32,768]{3,2,1,0:T(8,128)} %copy-done.1, f32[4,32,768]{2,1,0:T(8,128)} %kern_ref.1, s32[4]{0:T(128)} %kpt.1, s32[16,16]{1,0:T(8,128)} %q.1, bf16[2,768,768]{2,1,0:T(8,128)(2,1)} %constant.8.clone.whi, ...), custom_call_target="tpu_custom_call" | custom-call | tf_op jit(solution)/shard_map/exchange/pallas_call | solution.py:111
Async XLA Ops:
  12.0 38.0 %copy-start = (f32[4,1,2,32,768]{4,3,2,1,0:T(8,128)}, f32[4,1,2,32,768]{4,3,2,1,0:T(8,128)S(1)}, u32[]{:S(2)}) copy-start(f32[4,1,2,32,768]{4,3,2,1,0:T(8,128)S(1)} %all-gather) | copy-start | bytes 2359300
  12.0 25.0 %collective-permute-start.1 = (f32[4,2,32,768]{3,2,1,0:T(8,128)S(1)}, f32[4,2,32,768]{3,2,1,0:T(8,128)S(1)}, u32[]{:S(2)}, u32[]{:S(2)}) collective-permute-start(f32[4,2,32,768]{3,2,1,0:T(8,128)S(1)} %bitcast.2), channel_id=1, source_target_pairs={{4,0},{8,4},{12,8},{16,12},{20,16},{24,20},{28,24},{32,28},{36,32}... | collective-permute-start | bytes 2359304 | tf_op jit(solution)/shard_map/ppermute | solution.py:107
  20.2 29.8 %collective-permute-start = (f32[4,2,32,768]{3,2,1,0:T(8,128)S(1)}, f32[4,2,32,768]{3,2,1,0:T(8,128)S(1)}, u32[]{:S(2)}, u32[]{:S(2)}) collective-permute-start(f32[4,2,32,768]{3,2,1,0:T(8,128)S(1)} %bitcast.3), channel_id=1, source_target_pairs={{0,4},{4,8},{8,12},{12,16},{16,20},{20,24},{24,28},{28,32},{32,36}... | collective-permute-start | bytes 2359304 | tf_op jit(solution)/shard_map/ppermute | solution.py:106
  37.0 12.9 %copy-start.1 = (f32[4,2,32,768]{3,2,1,0:T(8,128)}, f32[4,2,32,768]{3,2,1,0:T(8,128)S(1)}, u32[]{:S(2)}) copy-start(f32[4,2,32,768]{3,2,1,0:T(8,128)S(1)} %collective-permute-done.1.high_ref) | copy-start | bytes 2359300
  50.0 0.9 %copy-start.2 = (f32[4,2,32,768]{3,2,1,0:T(8,128)}, f32[4,2,32,768]{3,2,1,0:T(8,128)S(1)}, u32[]{:S(2)}) copy-start(f32[4,2,32,768]{3,2,1,0:T(8,128)S(1)} %collective-permute-done.low_ref) | copy-start | bytes 2359300
where the time goes:
time: 69.8 us; the launch traced here: 69.6 us
  waiting for transfers between devices  29.8 us (43%)
  Pallas kernels  18.7 us (27%)
  blocking collectives  12 us (17%)
  starting transfers between devices  8.19 us (12%)
  local copies, waits for them, and re-layouts  0.91 us (1%)
    pallas_call x1, Pallas kernels, local(): pl.pallas_call(kernel, out_shape=jax.ShapeDtypeStruct((2, X, YZ), f32), i...  18.7 us
    ppermute x1, waiting for transfers between devices, local(): lax.ppermute(rows, 'band', [((i + 1) % count, i) for i in range(count)])  16.8 us
    ppermute x1, waiting for transfers between devices, local(): lax.ppermute(rows, 'band', [(i, (i + 1) % count) for i in range(count)])  12.9 us
    all_gather x1, blocking collectives, local(): rows = lax.all_gather(orbitals[0, 0], 'kpt', axis=0, tiled=False)  12 us
    ppermute x1, starting transfers between devices, local(): lax.ppermute(rows, 'band', [((i + 1) % count, i) for i in range(count)])  8.19 us
  transfers between devices with their start and end apart: 2, of which 2 were waited for; matrix products, arithmetic and copies ran while one was open for 0% of the time, Pallas kernels for 0%

commit v1 on v0

v1 whole, which is shorter than its diff:
```python
import numpy as np, ml_dtypes
import jax, jax.numpy as jnp
from jax import lax
from jax.sharding import PartitionSpec as P
from jax.experimental import pallas as pl
from jax.experimental.pallas import tpu as pltpu

X, Y, Z = 32, 32, 24
YZ = Y * Z
H = YZ // 2
f32 = jnp.float32
bf16 = jnp.bfloat16
COMPUTE = True


def split_np(a):
    hi = a.astype(np.float32).astype(ml_dtypes.bfloat16)
    lo = (a - hi.astype(np.float64)).astype(np.float32).astype(ml_dtypes.bfloat16)
    return hi, lo


def tables():
    y = np.arange(Y // 2)[:, None, None, None]
    z = np.arange(Z)[None, :, None, None]
    m = np.arange(Y // 2)[None, None, :, None]
    kz = np.arange(Z)[None, None, None, :]
    blocks = []
    for odd in range(2):
        angle = 2 * np.pi * ((3 * y * (2 * m + odd) + 4 * z * kz) % 96) / 96
        c = np.cos(angle).reshape(H, H)
        s = np.sin(angle).reshape(H, H)
        blocks.append(np.block([[c, -s], [s, c]]))
    whi, wlo = split_np(np.stack(blocks + [blocks[1].T]))
    x = np.arange(X)
    angle = 2 * np.pi * ((x[:, None] * x[None, :]) % X) / X
    c = np.cos(angle)
    s = np.sin(angle)

    def pair(d):
        h, l = split_np(d)
        o = np.zeros_like(h)
        return np.block([[h, h, o, o], [o, o, h, h], [l, o, o, o], [o, o, l, o]]).astype(ml_dtypes.bfloat16)

    dx = np.stack([pair(np.block([[c, s], [-s, c]])), pair(np.block([[c, -s], [s, c]]))])
    perm = np.zeros((YZ, YZ), np.float32)
    for odd in range(2):
        for mm in range(Y // 2):
            for k in range(Z):
                perm[(2 * mm + odd) * Z + k, odd * H + mm * Z + k] = 1
    return whi, wlo, dx, perm.astype(ml_dtypes.bfloat16)


def split(a):
    hi = a.astype(bf16)
    return hi, (a - hi.astype(f32)).astype(bf16)


def dot(a, b):
    return jnp.dot(a, b, preferred_element_type=f32)


def three(a, whi, wlo):
    hi, lo = split(a)
    n = a.shape[0]
    p = dot(jnp.concatenate([hi, lo], 0), whi)
    return p[:n] + p[n:] + dot(hi, wlo)


def lanes(*a):
    return jnp.concatenate(a, 1)


def rows(*a):
    return jnp.concatenate(a, 0)


def xdft(a0, a1, d):
    h0, l0 = split(a0)
    h1, l1 = split(a1)
    o = dot(d, rows(h0, l0, h1, l1))
    return o[:64] + o[128:192], o[64:128] + o[192:]


def group(vis, first, count, kp, kfirst, whi, wlo, dx, acc, between):
    s_rows = []
    d_rows = []
    rr, ri = vis[0, 0], vis[0, 1]
    for g in range(count):
        vr, vi = vis[first + g, 0], vis[first + g, 1]
        pr = vr * rr + vi * ri
        pi = vr * ri - vi * rr
        s_rows.append(lanes(pr[:, :H] + pr[:, H:], pi[:, :H] + pi[:, H:]))
        d_rows.append(lanes(pr[:, :H] - pr[:, H:], pi[:, :H] - pi[:, H:]))
    ts = three(rows(*s_rows), whi[0], wlo[0])
    td = three(rows(*d_rows), whi[1], wlo[1])
    between(0)
    e_rows = []
    o_rows = []
    for g in range(0, count, 2):
        a = []
        for i in (g, g + 1):
            r = slice(i * X, i * X + X)
            a.append(rows(lanes(ts[r, :H], td[r, :H]), lanes(ts[r, H:], td[r, H:])))
        s0, s1 = xdft(a[0], a[1], dx[0])
        k0, k1 = kp[kfirst + g], kp[kfirst + g + 1]
        s0 = s0 * rows(k0, k0)
        s1 = s1 * rows(k1, k1)
        for q in xdft(s0, s1, dx[1]):
            e_rows.append(lanes(q[X:, :H], q[:X, :H]))
            o_rows.append(lanes(q[:X, H:], q[X:, H:]))
    between(1)
    ue = three(rows(*e_rows), whi[0], wlo[0])
    uo = three(rows(*o_rows), whi[2], wlo[2])
    between(2)
    for g in range(count):
        r = slice(g * X, g * X + X)
        ei, er, orr, oi = ue[r, :H], ue[r, H:], uo[r, :H], uo[r, H:]
        pr = lanes(er + orr, er - orr)
        pi = lanes(ei + oi, ei - oi)
        vr, vi = vis[first + g, 0], vis[first + g, 1]
        acc[0] += vr * pr - vi * pi
        acc[1] += vr * pi + vi * pr


def permute_k(kern, kp, kpt, q, place, perm):
    own = kpt[place[0]]
    k = rows(*[kern[q[own, kpt[p]]] for p in place]) * (-1.0 / (4 * X * Y * Z))
    a = k.astype(bf16)
    r = k - a.astype(f32)
    b = r.astype(bf16)
    c = (r - b.astype(f32)).astype(bf16)
    out = dot(a, perm) + dot(b, perm) + dot(c, perm)
    for j in range(4):
        kp[j] = out[j * X : (j + 1) * X]


def kernel(bands, orb, kern_in, kpt, q, whi_in, wlo_in, dx_in, perm_in, out,
           vis, kern, whi, wlo, dx, perm, kp, local_sem, send_sem, recv_sem):
    k = lax.axis_index("kpt")
    b = lax.axis_index("band")
    core = lax.rem(k, 2)
    half = lax.div(k, 2)
    partner = k + 1 - 2 * core
    opposite = k + 2 - 4 * half
    opposite_partner = partner + 2 - 4 * half
    low = lax.rem(b, 2)
    other = b + 1 - 2 * low
    up = lax.rem(b + 2, bands)
    down = lax.rem(b + bands - 2, bands)
    target = up + low * (down - up)
    origin = down + low * (up - down)

    def device(band, kpoint):
        return {"band": band, "kpt": kpoint}

    places = [device(other, k), device(other, opposite), device(b, partner)]
    barrier = pltpu.get_barrier_semaphore()
    for d in places + [device(origin, k)]:
        pl.semaphore_signal(barrier, inc=1, device_id=d, device_id_type=pl.DeviceIdType.MESH)

    loads = [pltpu.make_async_copy(s, t, local_sem.at[i]) for i, (s, t) in enumerate(
        [(orb, vis.at[0]), (kern_in, kern), (perm_in, perm), (dx_in, dx)]
        + [(s.at[i], t.at[i]) for i in range(3) for s, t in ((whi_in, whi), (wlo_in, wlo))])]
    for c in loads:
        c.start()
    pl.semaphore_wait(barrier, 4)

    def send(i, src, dst, d):
        return pltpu.make_async_remote_copy(src_ref=src, dst_ref=dst, send_sem=send_sem.at[i],
                                            recv_sem=recv_sem.at[i], device_id=d,
                                            device_id_type=pl.DeviceIdType.MESH)

    along_x = [send(2 * n + p, orb.at[p], vis.at[4 + 2 * n, p], places[n]) for p in range(2) for n in range(2)]
    along_y = [send(4 + 2 * n + p, vis.at[4 + 2 * n, p], vis.at[8 + 2 * n, p], device(target, k))
               for p in range(2) for n in range(2)]
    relay = [send(8 + n, vis.at[6 - 2 * n, half], vis.at[2, half], places[n]) for n in range(2)]
    arrived = [send(8, vis.at[6, half], vis.at[2, half], places[0]),
               send(9, vis.at[4, half], vis.at[2, 1 - half], places[1])]
    to_core = [send(10, orb, vis.at[1], places[2]),
               send(11, vis.at[4], vis.at[5], places[2]), send(12, vis.at[6], vis.at[7], places[2]),
               send(13, vis.at[2], vis.at[3], places[2])]
    last = [send(14 + 2 * n + p, vis.at[8 + 2 * n, p], vis.at[9 + 2 * n, p], places[2])
            for p in range(2) for n in range(2)]

    for c in along_x:
        c.start()
    to_core[0].start()
    for n in range(2):
        along_x[n].wait_recv()
        along_y[n].start()
    loads[1].wait()
    loads[2].wait()
    permute_k(kern, kp, kpt, q, [k, partner, opposite, opposite_partner], perm[...])
    for n in range(2, 4):
        along_x[n].wait_recv()
        along_y[n].start()
    for c in relay:
        c.start()
    to_core[1].start()
    to_core[2].start()
    for i in (0, 3, 4, 5, 6, 7, 8, 9):
        loads[i].wait()
    out[...] = jnp.zeros_like(out)
    to_core[1].wait_recv()
    to_core[2].wait_recv()

    def opposite_in():
        for c in arrived:
            c.wait_recv()
        to_core[3].start()

    def outer_in(which):
        for i in which:
            along_y[i].wait_recv()
            last[i].start()

    def first(i):
        if i == 0:
            opposite_in()

    def second(i):
        if i == 1:
            outer_in((0, 1))
        if i == 2:
            outer_in((2, 3))

    if COMPUTE:
        group(vis, 4, 4, kp, 0, whi, wlo, dx, out, first)
    else:
        first(0)
    to_core[0].wait_recv()
    to_core[3].wait_recv()
    if COMPUTE:
        group(vis, 0, 4, kp, 0, whi, wlo, dx, out, second)
    else:
        second(1)
        second(2)
    for c in last:
        c.wait_recv()
    if COMPUTE:
        group(vis, 8, 4, kp, 0, whi, wlo, dx, out, lambda i: None)
    for c in along_x + along_y + relay + to_core + last:
        c.wait_send()


def local(orbitals, screened_kernel, kpoint_index, q_index):
    whi, wlo, dx, perm = tables()
    vmem = pl.BlockSpec(memory_space=pltpu.VMEM)
    smem = pl.BlockSpec(memory_space=pltpu.SMEM)
    hbm = pl.BlockSpec(memory_space=pl.ANY)
    bands = lax.axis_size("band")
    out = pl.pallas_call(
        lambda *refs: kernel(bands, *refs),
        out_shape=jax.ShapeDtypeStruct((2, X, YZ), f32),
        in_specs=[hbm] * 2 + [smem] * 2 + [hbm] * 4,
        out_specs=vmem,
        scratch_shapes=[
            pltpu.VMEM((12, 2, X, YZ), f32),
            pltpu.VMEM((4, X, YZ), f32),
            pltpu.VMEM(whi.shape, bf16),
            pltpu.VMEM(wlo.shape, bf16),
            pltpu.VMEM(dx.shape, bf16),
            pltpu.VMEM(perm.shape, bf16),
            pltpu.VMEM((4, X, YZ), f32),
            pltpu.SemaphoreType.DMA((10,)),
            pltpu.SemaphoreType.DMA((18,)),
            pltpu.SemaphoreType.DMA((18,)),
        ],
        compiler_params=pltpu.CompilerParams(
            vmem_limit_bytes=60 << 20, collective_id=0, has_side_effects=True
        ),
        name="exchange",
    )(orbitals[0, 0], screened_kernel, kpoint_index, q_index, whi, wlo, dx, perm)
    return out[None, None]


def solution(mesh):
    return jax.shard_map(
        local,
        mesh=mesh,
        in_specs=(P("band", "kpt", None, None, None), P(), P(), P()),
        out_specs=P("band", "kpt", None, None, None),
        check_vma=False,
    )
```

time: 69.8 us -> 33.2 us (0.48)
  waiting for transfers between devices: 29.8 us -> 0 us
  Pallas kernels: 18.7 us -> 31 us
  blocking collectives: 12 us -> 0 us
  starting transfers between devices: 8.19 us -> 0 us
  local copies, waits for them, and re-layouts: 0.91 us -> 1.62 us
    ppermute x2 -> x0, waiting for transfers between devices: 29.8 us -> none  [the longest x1 16.8 us: local(): lax.ppermute(rows, 'band', [((i + 1) % count, i) for i in range(count)])]
    pallas_call x1, Pallas kernels: 18.7 us -> 31 us  [local(): pl.pallas_call(lambda *refs: kernel(bands, *refs), out_shape=jax.ShapeDty...]
    all_gather x1 -> x0, blocking collectives: 12 us -> none  [local(): rows = lax.all_gather(orbitals[0, 0], 'kpt', axis=0, tiled=False)]
    ppermute x2 -> x0, starting transfers between devices: 8.19 us -> none  [the longest x1 8.19 us: local(): lax.ppermute(rows, 'band', [((i + 1) % count, i) for i in range(count)])]
    unnamed x6 -> x1, local copies, waits for them, and re-layouts: 0.91 us -> 1.62 us
  transfers between devices with their start and end apart: 2 -> 0, of which waited for: 2 -> 0; matrix products, arithmetic and copies ran while one was open for 0% -> 0% of each run, Pallas kernels for 0% -> 0%
where the time goes in v1:
time: 33.2 us; the launch traced here: 32.7 us
  Pallas kernels  31 us (93%)
  local copies, waits for them, and re-layouts  1.62 us (5%)
    pallas_call x1, Pallas kernels, local(): pl.pallas_call(lambda *refs: kernel(bands, *refs), out_shape=jax.ShapeDty...  31 us
    unnamed x1, local copies, waits for them, and re-layouts  1.62 us

profile of v1, /device:TPU:1, one launch (start us, length us, event | category | flops | bytes accessed | tf_op | source)
XLA Modules:
  0.0 32.7 jit_solution(1277427856534470041)
XLA Ops:
  0.0 31.0 %exchange.1 = f32[2,32,768]{2,1,0:T(8,128)} custom-call(f32[2,32,768]{2,1,0:T(8,128)} %bitcast.3, f32[4,32,768]{2,1,0:T(8,128)} %refs_1_.1, s32[4]{0:T(128)} %refs_2_.1, s32[16,16]{1,0:T(8,128)} %refs_3_.1, bf16[3,768,768]{2,1,0:T(8,128)(2,1)} %constant.8.clone.refs_4_, bf16[3,768,768]{2,1,0:T(8,128)(2,1)} %constant.9.clone.refs_5_, ...), custom_call_target="tpu_custom_call" | custom-call | tf_op jit(solution)/shard_map/exchange/pallas_call | solution.py:252
  31.0 1.6 %copy.10 = f32[1,1,2,32,768]{4,3,2,1,0:T(8,128)} copy(f32[1,1,2,32,768]{4,3,2,1,0:T(8,128)} %bitcast.2) | data formatting | bytes 393216

commit v2 on v1

--- a/solution.py
+++ b/solution.py
@@ -81,12 +81,13 @@
     return o[:64] + o[128:192], o[64:128] + o[192:]
 
 
-def group(vis, first, count, kp, kfirst, whi, wlo, dx, acc, between):
+def group(vis, slots, kp, whi, wlo, dx, acc, between):
+    count = len(slots)
     s_rows = []
     d_rows = []
     rr, ri = vis[0, 0], vis[0, 1]
     for g in range(count):
-        vr, vi = vis[first + g, 0], vis[first + g, 1]
+        vr, vi = vis[slots[g], 0], vis[slots[g], 1]
         pr = vr * rr + vi * ri
         pi = vr * ri - vi * rr
         s_rows.append(lanes(pr[:, :H] + pr[:, H:], pi[:, :H] + pi[:, H:]))
@@ -102,7 +103,7 @@
             r = slice(i * X, i * X + X)
             a.append(rows(lanes(ts[r, :H], td[r, :H]), lanes(ts[r, H:], td[r, H:])))
         s0, s1 = xdft(a[0], a[1], dx[0])
-        k0, k1 = kp[kfirst + g], kp[kfirst + g + 1]
+        k0, k1 = kp[slots[g] % 4], kp[slots[g + 1] % 4]
         s0 = s0 * rows(k0, k0)
         s1 = s1 * rows(k1, k1)
         for q in xdft(s0, s1, dx[1]):
@@ -117,7 +118,7 @@
         ei, er, orr, oi = ue[r, :H], ue[r, H:], uo[r, :H], uo[r, H:]
         pr = lanes(er + orr, er - orr)
         pi = lanes(ei + oi, ei - oi)
-        vr, vi = vis[first + g, 0], vis[first + g, 1]
+        vr, vi = vis[slots[g], 0], vis[slots[g], 1]
         acc[0] += vr * pr - vi * pi
         acc[1] += vr * pi + vi * pr
 
@@ -135,7 +136,7 @@
 
 
 def kernel(bands, orb, kern_in, kpt, q, whi_in, wlo_in, dx_in, perm_in, out,
-           vis, kern, whi, wlo, dx, perm, kp, local_sem, send_sem, recv_sem):
+           vis, transit, kern, whi, wlo, dx, perm, kp, local_sem, send_sem, recv_sem, x_ready, y_ready):
     k = lax.axis_index("kpt")
     b = lax.axis_index("band")
     core = lax.rem(k, 2)
@@ -154,92 +155,173 @@
         return {"band": band, "kpt": kpoint}
 
     places = [device(other, k), device(other, opposite), device(b, partner)]
+    mesh_ids = pl.DeviceIdType.MESH
     barrier = pltpu.get_barrier_semaphore()
-    for d in places + [device(origin, k)]:
-        pl.semaphore_signal(barrier, inc=1, device_id=d, device_id_type=pl.DeviceIdType.MESH)
+    pl.semaphore_signal(barrier, inc=1, device_id=device(other, 1), device_id_type=mesh_ids)
+    pl.semaphore_signal(barrier, inc=1, device_id=device(other, 3), device_id_type=mesh_ids)
+
+    @pl.when(core == 0)
+    def _():
+        pl.semaphore_signal(barrier, inc=1, device_id=places[2], device_id_type=mesh_ids)
+
+    for d in (up, down):
+        pl.semaphore_signal(barrier, inc=1, device_id=device(d, 2 * half), device_id_type=mesh_ids)
 
     loads = [pltpu.make_async_copy(s, t, local_sem.at[i]) for i, (s, t) in enumerate(
         [(orb, vis.at[0]), (kern_in, kern), (perm_in, perm), (dx_in, dx)]
         + [(s.at[i], t.at[i]) for i in range(3) for s, t in ((whi_in, whi), (wlo_in, wlo))])]
-    for c in loads:
-        c.start()
-    pl.semaphore_wait(barrier, 4)
+    for c in loads[:3]:
+        c.start()
 
     def send(i, src, dst, d):
         return pltpu.make_async_remote_copy(src_ref=src, dst_ref=dst, send_sem=send_sem.at[i],
                                             recv_sem=recv_sem.at[i], device_id=d,
-                                            device_id_type=pl.DeviceIdType.MESH)
-
-    along_x = [send(2 * n + p, orb.at[p], vis.at[4 + 2 * n, p], places[n]) for p in range(2) for n in range(2)]
-    along_y = [send(4 + 2 * n + p, vis.at[4 + 2 * n, p], vis.at[8 + 2 * n, p], device(target, k))
-               for p in range(2) for n in range(2)]
-    relay = [send(8 + n, vis.at[6 - 2 * n, half], vis.at[2, half], places[n]) for n in range(2)]
-    arrived = [send(8, vis.at[6, half], vis.at[2, half], places[0]),
-               send(9, vis.at[4, half], vis.at[2, 1 - half], places[1])]
-    to_core = [send(10, orb, vis.at[1], places[2]),
-               send(11, vis.at[4], vis.at[5], places[2]), send(12, vis.at[6], vis.at[7], places[2]),
-               send(13, vis.at[2], vis.at[3], places[2])]
-    last = [send(14 + 2 * n + p, vis.at[8 + 2 * n, p], vis.at[9 + 2 * n, p], places[2])
-            for p in range(2) for n in range(2)]
-
-    for c in along_x:
-        c.start()
+                                            device_id_type=mesh_ids)
+
+    cuts = [pl.ds(0, X // 2), pl.ds(X // 2, X // 2)]
+    both = range(2)
+    pieces = [(0, cuts[0]), (1, cuts[0]), (1, cuts[1]), (0, cuts[1])]
+    along_x = [send(2 * c + n, orb.at[0, cuts[c]], vis.at[4 + 2 * n, 0, cuts[c]], places[n]) for c in both for n in both]
+    along_x += [send(4 + n, orb.at[1], vis.at[4 + 2 * n, 1], places[n]) for n in both]
+    along_y = [send(6 + n, vis.at[4 + 2 * n, 0, cuts[0]], vis.at[8 + 2 * n, 0, cuts[0]], device(target, k)) for n in both]
+    through = [send(8 + i, orb.at[p, cut], transit.at[i], device(origin, k)) for i, (p, cut) in enumerate(pieces[1:])]
+    onward = [[send(11 + 2 * i + n, transit.at[i], vis.at[8 + 2 * n, p, cut], places[n]) for n in both]
+              for i, (p, cut) in enumerate(pieces[1:])]
+    relay = [send(17 + n, vis.at[6 - 2 * n, half], vis.at[2, half], places[n]) for n in both]
+    arrived = [send(17, vis.at[6, half], vis.at[2, half], places[0]),
+               send(18, vis.at[4, half], vis.at[2, 1 - half], places[1])]
+    to_core = [send(19, orb, vis.at[1], places[2]),
+               send(20, vis.at[4], vis.at[5], places[2]), send(21, vis.at[6], vis.at[7], places[2]),
+               send(22, vis.at[2], vis.at[3], places[2])]
+    last = [[send(23 + 2 * i + n, vis.at[8 + 2 * n, p, cut], vis.at[9 + 2 * n, p, cut], places[2]) for n in both]
+            for i, (p, cut) in enumerate(pieces)]
+
+    first_ring = lax.div(b, 2) == 0
+    late_in = jnp.logical_and(first_ring, low == 0)
+
+    def unless(flag, work):
+        pl.when(jnp.logical_not(flag))(work)
+
+    def enter_y():
+        pl.semaphore_wait(barrier, 4)
+        for c in through:
+            c.start()
+
+    def tell_y():
+        pl.semaphore_signal(y_ready, inc=1, device_id=places[2], device_id_type=mesh_ids)
+
+    def hear_y():
+        pl.semaphore_wait(y_ready, 1)
+        for c in through:
+            c.start()
+
+    @pl.when(core == 1)
+    def _():
+        pl.semaphore_wait(barrier, 5)
+        pl.semaphore_signal(x_ready, inc=1, device_id=places[2], device_id_type=mesh_ids)
+
+    @pl.when(core == 0)
+    def _():
+        unless(first_ring, enter_y)
+        pl.semaphore_wait(x_ready, 1)
+        unless(first_ring, tell_y)
+
+    for c in along_x[:4]:
+        c.start()
+
+    @pl.when(core == 1)
+    def _():
+        unless(first_ring, hear_y)
+
     to_core[0].start()
-    for n in range(2):
-        along_x[n].wait_recv()
-        along_y[n].start()
+    for c in loads[3:]:
+        c.start()
+
+    def relay_y():
+        for n in both:
+            along_x[n].wait_recv()
+            along_y[n].start()
+
+    def outer_in():
+        for i in range(3):
+            for n in both:
+                onward[i][n].wait_recv()
+                last[1 + i][n].start()
+            if i == 0:
+                for n in both:
+                    along_y[n].wait_recv()
+                    last[0][n].start()
+        for group_of in last:
+            for c in group_of:
+                c.wait_recv()
+
     loads[1].wait()
     loads[2].wait()
     permute_k(kern, kp, kpt, q, [k, partner, opposite, opposite_partner], perm[...])
-    for n in range(2, 4):
-        along_x[n].wait_recv()
-        along_y[n].start()
-    for c in relay:
-        c.start()
-    to_core[1].start()
-    to_core[2].start()
+    for c in along_x[4:]:
+        c.start()
+    unless(first_ring, relay_y)
+    out[...] = jnp.zeros_like(out)
     for i in (0, 3, 4, 5, 6, 7, 8, 9):
         loads[i].wait()
-    out[...] = jnp.zeros_like(out)
-    to_core[1].wait_recv()
-    to_core[2].wait_recv()
-
-    def opposite_in():
-        for c in arrived:
-            c.wait_recv()
-        to_core[3].start()
-
-    def outer_in(which):
-        for i in which:
-            along_y[i].wait_recv()
-            last[i].start()
-
-    def first(i):
-        if i == 0:
-            opposite_in()
-
-    def second(i):
-        if i == 1:
-            outer_in((0, 1))
+    to_core[0].wait_recv()
+
+    def compute(slots, between):
+        if COMPUTE:
+            group(vis, slots, kp, whi, wlo, dx, out, between)
+        else:
+            for i in range(3):
+                between(i)
+
+    def nothing(i):
+        pass
+
+    compute([0, 1], nothing)
+
+    @pl.when(first_ring)
+    def _():
+        @pl.when(core == 0)
+        def _():
+            enter_y()
+            tell_y()
+
+        pl.when(core == 1)(hear_y)
+        relay_y()
+
+    for c in along_x[2:]:
+        c.wait_recv()
+    for n in both:
+        to_core[1 + n].start()
+    for c in relay:
+        c.start()
+    for i in range(3):
+        through[i].wait_recv()
+        for c in onward[i]:
+            c.start()
+    for n in both:
+        to_core[1 + n].wait_recv()
+
+    def during_other(i):
         if i == 2:
-            outer_in((2, 3))
-
-    if COMPUTE:
-        group(vis, 4, 4, kp, 0, whi, wlo, dx, out, first)
-    else:
-        first(0)
-    to_core[0].wait_recv()
+            for c in arrived:
+                c.wait_recv()
+            to_core[3].start()
+
+    compute([4, 5, 6, 7], during_other)
     to_core[3].wait_recv()
-    if COMPUTE:
-        group(vis, 0, 4, kp, 0, whi, wlo, dx, out, second)
-    else:
-        second(1)
-        second(2)
-    for c in last:
-        c.wait_recv()
-    if COMPUTE:
-        group(vis, 8, 4, kp, 0, whi, wlo, dx, out, lambda i: None)
-    for c in along_x + along_y + relay + to_core + last:
+
+    @pl.when(late_in)
+    def _():
+        compute([2, 3], nothing)
+        outer_in()
+        compute([8, 9, 10, 11], nothing)
+
+    @pl.when(jnp.logical_not(late_in))
+    def _():
+        outer_in()
+        compute([2, 3, 8, 9, 10, 11], nothing)
+
+    for c in along_x + along_y + through + relay + to_core + sum(onward + last, []):
         c.wait_send()
 
 
@@ -256,6 +338,7 @@
         out_specs=vmem,
         scratch_shapes=[
             pltpu.VMEM((12, 2, X, YZ), f32),
+            pltpu.VMEM((3, X // 2, YZ), f32),
             pltpu.VMEM((4, X, YZ), f32),
             pltpu.VMEM(whi.shape, bf16),
             pltpu.VMEM(wlo.shape, bf16),
@@ -263,8 +346,10 @@
             pltpu.VMEM(perm.shape, bf16),
             pltpu.VMEM((4, X, YZ), f32),
             pltpu.SemaphoreType.DMA((10,)),
-            pltpu.SemaphoreType.DMA((18,)),
-            pltpu.SemaphoreType.DMA((18,)),
+            pltpu.SemaphoreType.DMA((31,)),
+            pltpu.SemaphoreType.DMA((31,)),
+            pltpu.SemaphoreType.REGULAR,
+            pltpu.SemaphoreType.REGULAR,
         ],
         compiler_params=pltpu.CompilerParams(
             vmem_limit_bytes=60 << 20, collective_id=0, has_side_effects=True

time: 33.2 us -> 28.1 us (0.85); the launches traced: 32.7 us -> 27.9 us
  Pallas kernels: 31 us -> 26.3 us
    pallas_call x1, Pallas kernels: 31 us -> 26.3 us  [local(): pl.pallas_call(lambda *refs: kernel(bands, *refs), out_shape=jax.ShapeDty...]
where the time goes in v2:
time: 28.1 us; the launch traced here: 27.9 us
  Pallas kernels  26.3 us (94%)
  local copies, waits for them, and re-layouts  1.62 us (6%)
    pallas_call x1, Pallas kernels, local(): pl.pallas_call(lambda *refs: kernel(bands, *refs), out_shape=jax.ShapeDty...  26.3 us
    unnamed x1, local copies, waits for them, and re-layouts  1.62 us

profile of v2, /device:TPU:1, one launch (start us, length us, event | category | flops | bytes accessed | tf_op | source)
XLA Modules:
  0.0 27.9 jit_solution(286203450954280862)
XLA Ops:
  0.0 26.3 %exchange.1 = f32[2,32,768]{2,1,0:T(8,128)} custom-call(f32[2,32,768]{2,1,0:T(8,128)} %bitcast.3, f32[4,32,768]{2,1,0:T(8,128)} %refs_1_.1, s32[4]{0:T(128)} %refs_2_.1, s32[16,16]{1,0:T(8,128)} %refs_3_.1, bf16[3,768,768]{2,1,0:T(8,128)(2,1)} %constant.8.clone.refs_4_, bf16[3,768,768]{2,1,0:T(8,128)(2,1)} %constant.9.clone.refs_5_, ...), custom_call_target="tpu_custom_call" | custom-call | tf_op jit(solution)/shard_map/exchange/pallas_call | solution.py:334
  26.3 1.6 %copy.10 = f32[1,1,2,32,768]{4,3,2,1,0:T(8,128)} copy(f32[1,1,2,32,768]{4,3,2,1,0:T(8,128)} %bitcast.2) | data formatting | bytes 393216

commit v3 on v2

--- a/solution.py
+++ b/solution.py
@@ -11,6 +11,7 @@
 f32 = jnp.float32
 bf16 = jnp.bfloat16
 COMPUTE = True
+RELAYED = 1
 
 
 def split_np(a):
@@ -135,8 +136,8 @@
         kp[j] = out[j * X : (j + 1) * X]
 
 
-def kernel(bands, orb, kern_in, kpt, q, whi_in, wlo_in, dx_in, perm_in, out,
-           vis, transit, kern, whi, wlo, dx, perm, kp, local_sem, send_sem, recv_sem, x_ready, y_ready):
+def kernel(bands, orb, kern_in, kpt_in, q_in, whi_in, wlo_in, dx_in, perm_in, out,
+           vis, transit, kern, kpt, q, whi, wlo, dx, perm, kp, local_sem, send_sem, recv_sem, x_ready, up_ready, down_ready):
     k = lax.axis_index("kpt")
     b = lax.axis_index("band")
     core = lax.rem(k, 2)
@@ -164,13 +165,12 @@
     def _():
         pl.semaphore_signal(barrier, inc=1, device_id=places[2], device_id_type=mesh_ids)
 
-    for d in (up, down):
-        pl.semaphore_signal(barrier, inc=1, device_id=device(d, 2 * half), device_id_type=mesh_ids)
+    pl.semaphore_signal(barrier, inc=1, device_id=device(down, 2 * half), device_id_type=mesh_ids)
 
     loads = [pltpu.make_async_copy(s, t, local_sem.at[i]) for i, (s, t) in enumerate(
-        [(orb, vis.at[0]), (kern_in, kern), (perm_in, perm), (dx_in, dx)]
+        [(orb, vis.at[0]), (kern_in, kern), (perm_in, perm), (kpt_in, kpt), (q_in, q), (dx_in, dx)]
         + [(s.at[i], t.at[i]) for i in range(3) for s, t in ((whi_in, whi), (wlo_in, wlo))])]
-    for c in loads[:3]:
+    for c in loads[:5]:
         c.start()
 
     def send(i, src, dst, d):
@@ -180,40 +180,44 @@
 
     cuts = [pl.ds(0, X // 2), pl.ds(X // 2, X // 2)]
     both = range(2)
-    pieces = [(0, cuts[0]), (1, cuts[0]), (1, cuts[1]), (0, cuts[1])]
-    along_x = [send(2 * c + n, orb.at[0, cuts[c]], vis.at[4 + 2 * n, 0, cuts[c]], places[n]) for c in both for n in both]
-    along_x += [send(4 + n, orb.at[1], vis.at[4 + 2 * n, 1], places[n]) for n in both]
-    along_y = [send(6 + n, vis.at[4 + 2 * n, 0, cuts[0]], vis.at[8 + 2 * n, 0, cuts[0]], device(target, k)) for n in both]
-    through = [send(8 + i, orb.at[p, cut], transit.at[i], device(origin, k)) for i, (p, cut) in enumerate(pieces[1:])]
-    onward = [[send(11 + 2 * i + n, transit.at[i], vis.at[8 + 2 * n, p, cut], places[n]) for n in both]
-              for i, (p, cut) in enumerate(pieces[1:])]
-    relay = [send(17 + n, vis.at[6 - 2 * n, half], vis.at[2, half], places[n]) for n in both]
-    arrived = [send(17, vis.at[6, half], vis.at[2, half], places[0]),
-               send(18, vis.at[4, half], vis.at[2, 1 - half], places[1])]
-    to_core = [send(19, orb, vis.at[1], places[2]),
-               send(20, vis.at[4], vis.at[5], places[2]), send(21, vis.at[6], vis.at[7], places[2]),
-               send(22, vis.at[2], vis.at[3], places[2])]
-    last = [[send(23 + 2 * i + n, vis.at[8 + 2 * n, p, cut], vis.at[9 + 2 * n, p, cut], places[2]) for n in both]
-            for i, (p, cut) in enumerate(pieces)]
+    pieces = [(0, cuts[0]), (0, cuts[1]), (1, cuts[0]), (1, cuts[1])]
+    relayed, routed = pieces[:RELAYED], pieces[RELAYED:]
+    index = iter(range(31))
+    along_x = [[send(next(index), orb.at[0, cuts[c]], vis.at[4 + 2 * n, 0, cuts[c]], places[n]) for n in both]
+               for c in both]
+    along_x += [[send(next(index), orb.at[1], vis.at[4 + 2 * n, 1], places[n]) for n in both]]
+    along_y = [[send(next(index), vis.at[4 + 2 * n, p, cut], vis.at[8 + 2 * n, p, cut], device(target, k)) for n in both]
+               for p, cut in relayed]
+    through = [send(next(index), orb.at[p, cut], transit.at[i], device(origin, k)) for i, (p, cut) in enumerate(routed)]
+    onward = [[send(next(index), transit.at[i], vis.at[8 + 2 * n, p, cut], places[n]) for n in both]
+              for i, (p, cut) in enumerate(routed)]
+    first = next(index)
+    second = next(index)
+    relay = [send(first, vis.at[6, half], vis.at[2, half], places[0]),
+             send(second, vis.at[4, half], vis.at[2, half], places[1])]
+    arrived = [send(first, vis.at[6, half], vis.at[2, half], places[0]),
+               send(second, vis.at[4, half], vis.at[2, 1 - half], places[1])]
+    to_core = [send(next(index), orb, vis.at[1], places[2]),
+               send(next(index), vis.at[4], vis.at[5], places[2]), send(next(index), vis.at[6], vis.at[7], places[2]),
+               send(next(index), vis.at[2], vis.at[3], places[2])]
+    last = [[send(next(index), vis.at[8 + 2 * n, p, cut], vis.at[9 + 2 * n, p, cut], places[2]) for n in both]
+            for p, cut in pieces]
 
     first_ring = lax.div(b, 2) == 0
     late_in = jnp.logical_and(first_ring, low == 0)
+    late_relay = jnp.logical_and(first_ring, low == 1)
+    late_through = jnp.logical_or(late_relay, b == bands - 2)
 
     def unless(flag, work):
         pl.when(jnp.logical_not(flag))(work)
 
-    def enter_y():
-        pl.semaphore_wait(barrier, 4)
+    def route():
         for c in through:
             c.start()
 
-    def tell_y():
-        pl.semaphore_signal(y_ready, inc=1, device_id=places[2], device_id_type=mesh_ids)
-
-    def hear_y():
-        pl.semaphore_wait(y_ready, 1)
-        for c in through:
-            c.start()
+    def hear_down():
+        pl.semaphore_wait(down_ready, 1)
+        pl.when(low == 0)(route)
 
     @pl.when(core == 1)
     def _():
@@ -222,48 +226,52 @@
 
     @pl.when(core == 0)
     def _():
-        unless(first_ring, enter_y)
+        pl.semaphore_wait(barrier, 2)
+        pl.when(low == 1)(route)
         pl.semaphore_wait(x_ready, 1)
-        unless(first_ring, tell_y)
-
-    for c in along_x[:4]:
+        pl.semaphore_signal(up_ready, inc=1, device_id=places[2], device_id_type=mesh_ids)
+        for kpoint in (k, partner):
+            pl.semaphore_signal(down_ready, inc=1, device_id=device(up, kpoint), device_id_type=mesh_ids)
+
+    for c in sum(along_x, []):
         c.start()
 
     @pl.when(core == 1)
     def _():
-        unless(first_ring, hear_y)
+        pl.semaphore_wait(up_ready, 1)
+        pl.when(low == 1)(route)
 
     to_core[0].start()
-    for c in loads[3:]:
+    for c in loads[5:]:
         c.start()
 
-    def relay_y():
+    def relay_y(arrive, leave):
+        for i in range(len(relayed)):
+            for n in both:
+                if arrive:
+                    along_x[i][n].wait_recv()
+                if leave:
+                    along_y[i][n].start()
+
+    def pass_on(i):
+        through[i].wait_recv()
+        for c in onward[i]:
+            c.start()
+
+    def outer_in(i):
         for n in both:
-            along_x[n].wait_recv()
-            along_y[n].start()
-
-    def outer_in():
-        for i in range(3):
-            for n in both:
-                onward[i][n].wait_recv()
-                last[1 + i][n].start()
-            if i == 0:
-                for n in both:
-                    along_y[n].wait_recv()
-                    last[0][n].start()
-        for group_of in last:
-            for c in group_of:
-                c.wait_recv()
-
-    loads[1].wait()
-    loads[2].wait()
+            (along_y + onward)[i][n].wait_recv()
+            last[i][n].start()
+
+    for c in loads[1:5]:
+        c.wait()
     permute_k(kern, kp, kpt, q, [k, partner, opposite, opposite_partner], perm[...])
-    for c in along_x[4:]:
-        c.start()
-    unless(first_ring, relay_y)
+    unless(first_ring, hear_down)
+    unless(late_relay, lambda: relay_y(True, True))
     out[...] = jnp.zeros_like(out)
-    for i in (0, 3, 4, 5, 6, 7, 8, 9):
-        loads[i].wait()
+    loads[0].wait()
+    for c in loads[5:]:
+        c.wait()
     to_core[0].wait_recv()
 
     def compute(slots, between):
@@ -276,86 +284,106 @@
     def nothing(i):
         pass
 
-    compute([0, 1], nothing)
-
-    @pl.when(first_ring)
-    def _():
-        @pl.when(core == 0)
-        def _():
-            enter_y()
-            tell_y()
-
-        pl.when(core == 1)(hear_y)
-        relay_y()
-
-    for c in along_x[2:]:
-        c.wait_recv()
+    def during_own(i):
+        if i != 1:
+            unless(late_through, lambda: pass_on(i // 2))
+
+    compute([0, 1], during_own)
+
+    pl.when(late_relay)(lambda: relay_y(True, False))
+    for i in range(len(relayed), 3):
+        for c in along_x[i]:
+            c.wait_recv()
     for n in both:
         to_core[1 + n].start()
     for c in relay:
         c.start()
-    for i in range(3):
-        through[i].wait_recv()
-        for c in onward[i]:
-            c.start()
+
+    pl.when(first_ring)(hear_down)
+    pl.when(late_relay)(lambda: relay_y(False, True))
+
+    @pl.when(late_through)
+    def _():
+        pass_on(0)
+        pass_on(1)
+
+    for i in range(2, len(routed)):
+        pass_on(i)
     for n in both:
         to_core[1 + n].wait_recv()
 
     def during_other(i):
+        if i == 0:
+            unless(late_in, lambda: outer_in(0))
+        if i == 1:
+            unless(late_in, lambda: outer_in(1))
         if i == 2:
-            for c in arrived:
-                c.wait_recv()
-            to_core[3].start()
+            unless(late_in, lambda: outer_in(2))
 
     compute([4, 5, 6, 7], during_other)
-    to_core[3].wait_recv()
+    for c in arrived:
+        c.wait_recv()
+    to_core[3].start()
 
     @pl.when(late_in)
     def _():
+        to_core[3].wait_recv()
         compute([2, 3], nothing)
-        outer_in()
+        for i in (1, 0, 2, 3):
+            outer_in(i)
+        for c in sum(last, []):
+            c.wait_recv()
         compute([8, 9, 10, 11], nothing)
 
     @pl.when(jnp.logical_not(late_in))
     def _():
-        outer_in()
+        outer_in(3)
+        to_core[3].wait_recv()
+        for c in sum(last, []):
+            c.wait_recv()
         compute([2, 3, 8, 9, 10, 11], nothing)
 
-    for c in along_x + along_y + through + relay + to_core + sum(onward + last, []):
+    for c in sum(along_x + along_y + onward + last, []) + through + relay + to_core:
         c.wait_send()
+
+
+def pin(a):
+    return pltpu.with_memory_space_constraint(jnp.asarray(a), pltpu.HBM)
 
 
 def local(orbitals, screened_kernel, kpoint_index, q_index):
     whi, wlo, dx, perm = tables()
     vmem = pl.BlockSpec(memory_space=pltpu.VMEM)
-    smem = pl.BlockSpec(memory_space=pltpu.SMEM)
     hbm = pl.BlockSpec(memory_space=pl.ANY)
     bands = lax.axis_size("band")
     out = pl.pallas_call(
         lambda *refs: kernel(bands, *refs),
         out_shape=jax.ShapeDtypeStruct((2, X, YZ), f32),
-        in_specs=[hbm] * 2 + [smem] * 2 + [hbm] * 4,
+        in_specs=[hbm] * 8,
         out_specs=vmem,
         scratch_shapes=[
             pltpu.VMEM((12, 2, X, YZ), f32),
-            pltpu.VMEM((3, X // 2, YZ), f32),
+            pltpu.VMEM((4 - RELAYED, X // 2, YZ), f32),
             pltpu.VMEM((4, X, YZ), f32),
+            pltpu.SMEM(kpoint_index.shape, jnp.int32),
+            pltpu.SMEM(q_index.shape, jnp.int32),
             pltpu.VMEM(whi.shape, bf16),
             pltpu.VMEM(wlo.shape, bf16),
             pltpu.VMEM(dx.shape, bf16),
             pltpu.VMEM(perm.shape, bf16),
             pltpu.VMEM((4, X, YZ), f32),
-            pltpu.SemaphoreType.DMA((10,)),
+            pltpu.SemaphoreType.DMA((12,)),
             pltpu.SemaphoreType.DMA((31,)),
             pltpu.SemaphoreType.DMA((31,)),
             pltpu.SemaphoreType.REGULAR,
             pltpu.SemaphoreType.REGULAR,
+            pltpu.SemaphoreType.REGULAR,
         ],
         compiler_params=pltpu.CompilerParams(
-            vmem_limit_bytes=60 << 20, collective_id=0, has_side_effects=True
+            vmem_limit_bytes=30 << 20, collective_id=0, has_side_effects=True
         ),
         name="exchange",
-    )(orbitals[0, 0], screened_kernel, kpoint_index, q_index, whi, wlo, dx, perm)
+    )(*map(pin, (orbitals[0, 0], screened_kernel, kpoint_index, q_index, whi, wlo, dx, perm)))
     return out[None, None]
 
 

time: 28.1 us -> 25.8 us (0.918)
  Pallas kernels: 26.3 us -> 25 us
  local copies, waits for them, and re-layouts: 1.62 us -> 0.68 us
    pallas_call x1, Pallas kernels: 26.3 us -> 25 us  [local(): pl.pallas_call(lambda *refs: kernel(bands, *refs), out_shape=jax.ShapeDty...]
    unnamed x1, local copies, waits for them, and re-layouts: 1.62 us -> 0.68 us
where the time goes in v3:
time: 25.8 us; the launch traced here: 25.7 us
  Pallas kernels  25 us (97%)
  local copies, waits for them, and re-layouts  0.68 us (3%)
    pallas_call x1, Pallas kernels, local(): pl.pallas_call(lambda *refs: kernel(bands, *refs), out_shape=jax.ShapeDty...  25 us
    unnamed x1, local copies, waits for them, and re-layouts  0.68 us

profile of v3, /device:TPU:1, one launch (start us, length us, event | category | flops | bytes accessed | tf_op | source)
XLA Modules:
  0.0 25.7 jit_solution(9633997778425273073)
XLA Ops:
  0.0 25.0 %exchange.1 = f32[2,32,768]{2,1,0:T(8,128)S(1)} custom-call(f32[2,32,768]{2,1,0:T(8,128)} %bitcast.3, f32[4,32,768]{2,1,0:T(8,128)} %refs_1_.1, s32[4]{0:T(128)} %refs_2_.1, s32[16,16]{1,0:T(8,128)} %refs_3_.1, bf16[3,768,768]{2,1,0:T(8,128)(2,1)} %constant.8.clone.refs_4_, bf16[3,768,768]{2,1,0:T(8,128)(2,1)} %constant.9.clone.refs_5_, ...), custom_call_target="tpu_custom_call" | custom-call | tf_op jit(solution)/shard_map/exchange/pallas_call | solution.py:359
  25.0 0.7 %copy.10 = f32[1,1,2,32,768]{4,3,2,1,0:T(8,128)} copy(f32[1,1,2,32,768]{4,3,2,1,0:T(8,128)S(1)} %bitcast.2) | data formatting | bytes 393216

commit v4 on v3

--- a/solution.py
+++ b/solution.py
@@ -182,7 +182,7 @@
     both = range(2)
     pieces = [(0, cuts[0]), (0, cuts[1]), (1, cuts[0]), (1, cuts[1])]
     relayed, routed = pieces[:RELAYED], pieces[RELAYED:]
-    index = iter(range(31))
+    index = iter(range(33))
     along_x = [[send(next(index), orb.at[0, cuts[c]], vis.at[4 + 2 * n, 0, cuts[c]], places[n]) for n in both]
                for c in both]
     along_x += [[send(next(index), orb.at[1], vis.at[4 + 2 * n, 1], places[n]) for n in both]]
@@ -198,8 +198,9 @@
     arrived = [send(first, vis.at[6, half], vis.at[2, half], places[0]),
                send(second, vis.at[4, half], vis.at[2, 1 - half], places[1])]
     to_core = [send(next(index), orb, vis.at[1], places[2]),
-               send(next(index), vis.at[4], vis.at[5], places[2]), send(next(index), vis.at[6], vis.at[7], places[2]),
                send(next(index), vis.at[2], vis.at[3], places[2])]
+    other_to_core = [[send(next(index), vis.at[4 + 2 * n, p], vis.at[5 + 2 * n, p], places[2]) for n in both]
+                     for p in both]
     last = [[send(next(index), vis.at[8 + 2 * n, p, cut], vis.at[9 + 2 * n, p, cut], places[2]) for n in both]
             for p, cut in pieces]
 
@@ -285,65 +286,73 @@
         pass
 
     def during_own(i):
-        if i != 1:
-            unless(late_through, lambda: pass_on(i // 2))
+        if i == 2:
+            pl.when(late_relay)(lambda: relay_y(True, False))
+            for r in range(len(relayed), 2):
+                for c in along_x[r]:
+                    c.wait_recv()
+            for c in other_to_core[0]:
+                c.start()
+            unless(late_through, lambda: pass_on(0))
 
     compute([0, 1], during_own)
 
-    pl.when(late_relay)(lambda: relay_y(True, False))
-    for i in range(len(relayed), 3):
-        for c in along_x[i]:
-            c.wait_recv()
-    for n in both:
-        to_core[1 + n].start()
+    for c in along_x[2]:
+        c.wait_recv()
+    for c in other_to_core[1]:
+        c.start()
     for c in relay:
         c.start()
 
     pl.when(first_ring)(hear_down)
     pl.when(late_relay)(lambda: relay_y(False, True))
 
-    @pl.when(late_through)
-    def _():
-        pass_on(0)
-        pass_on(1)
-
-    for i in range(2, len(routed)):
-        pass_on(i)
-    for n in both:
-        to_core[1 + n].wait_recv()
+    for c in sum(other_to_core, []):
+        c.wait_recv()
 
     def during_other(i):
         if i == 0:
-            unless(late_in, lambda: outer_in(0))
-        if i == 1:
-            unless(late_in, lambda: outer_in(1))
+            @pl.when(late_through)
+            def _():
+                for r in range(len(routed)):
+                    pass_on(r)
+
+            @pl.when(jnp.logical_not(late_through))
+            def _():
+                for r in range(1, len(routed)):
+                    pass_on(r)
+
         if i == 2:
-            unless(late_in, lambda: outer_in(2))
+            for c in arrived:
+                c.wait_recv()
+            to_core[1].start()
+
+            @pl.when(jnp.logical_not(late_in))
+            def _():
+                for r in range(len(relayed) + 1):
+                    outer_in(r)
 
     compute([4, 5, 6, 7], during_other)
-    for c in arrived:
-        c.wait_recv()
-    to_core[3].start()
+    to_core[1].wait_recv()
+
+    def during_opposite(i):
+        if i == 2:
+            @pl.when(jnp.logical_not(late_in))
+            def _():
+                for r in range(len(relayed) + 1, 4):
+                    outer_in(r)
+
+    compute([2, 3], during_opposite)
 
     @pl.when(late_in)
     def _():
-        to_core[3].wait_recv()
-        compute([2, 3], nothing)
         for i in (1, 0, 2, 3):
             outer_in(i)
-        for c in sum(last, []):
-            c.wait_recv()
-        compute([8, 9, 10, 11], nothing)
-
-    @pl.when(jnp.logical_not(late_in))
-    def _():
-        outer_in(3)
-        to_core[3].wait_recv()
-        for c in sum(last, []):
-            c.wait_recv()
-        compute([2, 3, 8, 9, 10, 11], nothing)
-
-    for c in sum(along_x + along_y + onward + last, []) + through + relay + to_core:
+
+    for c in sum(last, []):
+        c.wait_recv()
+    compute([8, 9, 10, 11], nothing)
+    for c in sum(along_x + along_y + onward + last + other_to_core, []) + through + relay + to_core:
         c.wait_send()
 
 
@@ -373,8 +382,8 @@
             pltpu.VMEM(perm.shape, bf16),
             pltpu.VMEM((4, X, YZ), f32),
             pltpu.SemaphoreType.DMA((12,)),
-            pltpu.SemaphoreType.DMA((31,)),
-            pltpu.SemaphoreType.DMA((31,)),
+            pltpu.SemaphoreType.DMA((33,)),
+            pltpu.SemaphoreType.DMA((33,)),
             pltpu.SemaphoreType.REGULAR,
             pltpu.SemaphoreType.REGULAR,
             pltpu.SemaphoreType.REGULAR,

time: 25.8 us -> 25.1 us (0.973)
  Pallas kernels: 25 us -> 24.3 us
    pallas_call x1, Pallas kernels: 25 us -> 24.3 us  [local(): pl.pallas_call(lambda *refs: kernel(bands, *refs), out_shape=jax.ShapeDty...]
where the time goes in v4:
time: 25.1 us; the launch traced here: 25 us
  Pallas kernels  24.3 us (97%)
  local copies, waits for them, and re-layouts  0.68 us (3%)
    pallas_call x1, Pallas kernels, local(): pl.pallas_call(lambda *refs: kernel(bands, *refs), out_shape=jax.ShapeDty...  24.3 us
    unnamed x1, local copies, waits for them, and re-layouts  0.68 us

profile of v4, /device:TPU:1, one launch (start us, length us, event | category | flops | bytes accessed | tf_op | source)
XLA Modules:
  0.0 25.0 jit_solution(14382912934811749128)
XLA Ops:
  0.0 24.3 %exchange.1 = f32[2,32,768]{2,1,0:T(8,128)S(1)} custom-call(f32[2,32,768]{2,1,0:T(8,128)} %bitcast.3, f32[4,32,768]{2,1,0:T(8,128)} %refs_1_.1, s32[4]{0:T(128)} %refs_2_.1, s32[16,16]{1,0:T(8,128)} %refs_3_.1, bf16[3,768,768]{2,1,0:T(8,128)(2,1)} %constant.8.clone.refs_4_, bf16[3,768,768]{2,1,0:T(8,128)(2,1)} %constant.9.clone.refs_5_, ...), custom_call_target="tpu_custom_call" | custom-call | tf_op jit(solution)/shard_map/exchange/pallas_call | solution.py:368
  24.3 0.7 %copy.10 = f32[1,1,2,32,768]{4,3,2,1,0:T(8,128)} copy(f32[1,1,2,32,768]{4,3,2,1,0:T(8,128)S(1)} %bitcast.2) | data formatting | bytes 393216

commit v5 on v4

--- a/solution.py
+++ b/solution.py
@@ -114,14 +114,17 @@
     ue = three(rows(*e_rows), whi[0], wlo[0])
     uo = three(rows(*o_rows), whi[2], wlo[2])
     between(2)
+    re, im = acc[0], acc[1]
     for g in range(count):
         r = slice(g * X, g * X + X)
         ei, er, orr, oi = ue[r, :H], ue[r, H:], uo[r, :H], uo[r, H:]
         pr = lanes(er + orr, er - orr)
         pi = lanes(ei + oi, ei - oi)
         vr, vi = vis[slots[g], 0], vis[slots[g], 1]
-        acc[0] += vr * pr - vi * pi
-        acc[1] += vr * pi + vi * pr
+        re = re + (vr * pr - vi * pi)
+        im = im + (vr * pi + vi * pr)
+    acc[0] = re
+    acc[1] = im
 
 
 def permute_k(kern, kp, kpt, q, place, perm):
@@ -349,10 +352,12 @@
         for i in (1, 0, 2, 3):
             outer_in(i)
 
+    for c in sum(along_x + along_y + onward + other_to_core, []) + through + relay + to_core:
+        c.wait_send()
     for c in sum(last, []):
         c.wait_recv()
     compute([8, 9, 10, 11], nothing)
-    for c in sum(along_x + along_y + onward + last + other_to_core, []) + through + relay + to_core:
+    for c in sum(last, []):
         c.wait_send()
 
 

time: 25.1 us -> 25 us (level)
  no operation moved by 1% of the time
where the time goes in v5:
time: 25 us; the launch traced here: 24.9 us
  Pallas kernels  24.2 us (97%)
  local copies, waits for them, and re-layouts  0.68 us (3%)
    pallas_call x1, Pallas kernels, local(): pl.pallas_call(lambda *refs: kernel(bands, *refs), out_shape=jax.ShapeDty...  24.2 us
    unnamed x1, local copies, waits for them, and re-layouts  0.68 us

profile of v5, /device:TPU:1, one launch (start us, length us, event | category | flops | bytes accessed | tf_op | source)
XLA Modules:
  0.0 24.9 jit_solution(16470575388842616731)
XLA Ops:
  0.0 24.2 %exchange.1 = f32[2,32,768]{2,1,0:T(8,128)S(1)} custom-call(f32[2,32,768]{2,1,0:T(8,128)} %bitcast.3, f32[4,32,768]{2,1,0:T(8,128)} %refs_1_.1, s32[4]{0:T(128)} %refs_2_.1, s32[16,16]{1,0:T(8,128)} %refs_3_.1, bf16[3,768,768]{2,1,0:T(8,128)(2,1)} %constant.8.clone.refs_4_, bf16[3,768,768]{2,1,0:T(8,128)(2,1)} %constant.9.clone.refs_5_, ...), custom_call_target="tpu_custom_call" | custom-call | tf_op jit(solution)/shard_map/exchange/pallas_call | solution.py:373
  24.2 0.7 %copy.10 = f32[1,1,2,32,768]{4,3,2,1,0:T(8,128)} copy(f32[1,1,2,32,768]{4,3,2,1,0:T(8,128)S(1)} %bitcast.2) | data formatting | bytes 393216
